TPU v7x, 32 devices: a whole 2x2x4 slice. The times are simulated.
32 devices in a mesh: band: 8 (over z, y), ga: 4 (over x, core).
Axes of the slice: x: 2, y: 2, z: 4, core: 2. Of those that a mesh axis runs over, the one named last changes fastest.
Arguments:
- valence: bfloat16 [8, 2, 128, 128, 128], P('band', None, 'ga'), may hold values from -6 to 6
- conduction: bfloat16 [48, 128, 128, 128], P('band', 'ga'), may hold values from -6 to 6
- owners: int32 [2], replicated, may hold values from 0 to 7
- val_energy: float32 [2], replicated, may hold values from -8 to -4
- cond_energy: float32 [48], P('band'), may hold values from 0.5 to 20
- gvec_index: int32 [1280], P('ga'), may hold values from 0 to 65535, as said below
Outputs:
- chi_panel: float32 [1280, 512], P('band', 'ga')
Inputs may be any that keep to these rules, and one draw needn't show every extreme that they name: owners[k] is the band group whose slot k holds valence band k. `gvec_index`: within each block j of 320 entries the values are distinct; value a 1024 + b * 64 + c names x-frequency index a, y-frequency index j * 16 + b, z-frequency index c.
All inputs are finite; a program needn't handle non-finite values.
Results may differ from a plain program's by a relative error of at most 0.0048.
Values may be sent and summed in bfloat16 or wider, within the bound.
No kernel may reach another device: no remote copies, remote signals or barrier semaphores. Data moves between devices by JAX's collectives and lax.ppermute only.
A program may use at most 128 MiB of HBM per device.

v0:
```python
import math

import jax
import jax.numpy as jnp
from jax import lax
from jax.sharding import PartitionSpec as P

NGRID = 128
KB = 64
NV = 2
PANEL_DEV = 128


highest = lax.Precision.HIGHEST


def spread_2(block, axis, holder):
    block = jnp.where(lax.axis_index(axis) == holder, block, jnp.zeros_like(block))
    return lax.psum(block, axis)


def dft_tables(grid_count, freq_count):
    grid_points = jnp.arange(grid_count, dtype=jnp.int32)
    shifted = jnp.arange(freq_count, dtype=jnp.int32) - freq_count // 2
    phase_index = grid_points[:, None] * shifted[None, :] % grid_count
    angles = phase_index.astype(jnp.float32) * (2.0 * math.pi / grid_count)
    scale_factor = 1.0 / math.sqrt(grid_count)
    return (jnp.cos(angles) * scale_factor, -jnp.sin(angles) * scale_factor)


def front_half(fields, cosine_table, sine_table, freq_count):
    both_tables = jnp.concatenate([cosine_table, sine_table], axis=1)
    zpart = jnp.einsum("fxyz,zq->fxyq", fields, both_tables, precision=highest)
    real_z, imag_z = (zpart[..., :freq_count], zpart[..., freq_count:])
    real_y = jnp.einsum("fxyk,yq->fxqk", real_z, cosine_table, precision=highest) - jnp.einsum(
        "fxyk,yq->fxqk", imag_z, sine_table, precision=highest
    )
    imag_y = jnp.einsum("fxyk,yq->fxqk", imag_z, cosine_table, precision=highest) + jnp.einsum(
        "fxyk,yq->fxqk", real_z, sine_table, precision=highest
    )
    return jnp.concatenate([real_y, imag_y], axis=-1)


def back_half(arrived, cosine_table, sine_table, freq_count):
    real_y, imag_y = (arrived[..., :freq_count], arrived[..., freq_count:])
    real_x = jnp.einsum("fxjk,xq->fqjk", real_y, cosine_table, precision=highest) - jnp.einsum(
        "fxjk,xq->fqjk", imag_y, sine_table, precision=highest
    )
    imag_x = jnp.einsum("fxjk,xq->fqjk", imag_y, cosine_table, precision=highest) + jnp.einsum(
        "fxjk,xq->fqjk", real_y, sine_table, precision=highest
    )
    return jnp.concatenate([real_x, imag_x], axis=-1)


def per_device(valence, conduction, owners, val_energy, cond_energy, gvec_index):
    cosine_table, sine_table = dft_tables(NGRID, KB)
    local_val = valence[0]
    waves = conduction.astype(jnp.float32)
    spectra_list = []
    for band_slot in range(NV):
        val_field = spread_2(local_val[band_slot], "band", owners[band_slot]).astype(jnp.float32)
        fields = waves * val_field[None]
        partial_value = front_half(fields, cosine_table, sine_table, KB)
        arrived = lax.all_to_all(partial_value, "ga", split_axis=2, concat_axis=1, tiled=True)
        spectra_list.append(back_half(arrived, cosine_table, sine_table, KB))
    spectra = jnp.concatenate(spectra_list, axis=0)
    field_count = spectra.shape[0]
    kyd_local = spectra.shape[2]
    arranged = (
        spectra.reshape(field_count, KB, kyd_local, 2, KB)
        .transpose(0, 3, 1, 2, 4)
        .reshape(field_count, 2, -1)
    )
    picked = arranged[:, :, gvec_index]
    coeffs = picked.reshape(field_count * 2, -1).astype(jnp.bfloat16)
    weights = 1.0 / (val_energy[:, None] - cond_energy[None, :])
    col_weights = jnp.repeat(weights.reshape(-1), 2)
    weighted = (coeffs[:, :PANEL_DEV].astype(jnp.float32) * col_weights[:, None]).astype(
        jnp.bfloat16
    )
    gathered = lax.all_gather(coeffs, "ga", axis=1, tiled=True)
    contract = (((0,), (0,)), ((), ()))
    row_coeffs = lax.all_to_all(gathered, "band", split_axis=1, concat_axis=0, tiled=True)
    panel_all = lax.all_gather(weighted, "band", axis=0, tiled=True)
    chi_block = lax.dot_general(row_coeffs, panel_all, contract, preferred_element_type=jnp.float32)
    return chi_block


def solution(mesh):
    in_specs = (
        P("band", None, "ga", None, None),
        P("band", "ga", None, None),
        P(),
        P(),
        P("band"),
        P("ga"),
    )
    out_specs = P("band", "ga")
    return jax.shard_map(
        per_device, mesh=mesh, in_specs=in_specs, out_specs=out_specs, check_vma=False
    )
```

profile of v0, /device:TPU:0, one launch (start us, length us, event | category | flops | bytes accessed | tf_op | source)
XLA Modules:
  0.0 626.9 jit_solution(12723096447552680584)
XLA Ops:
  6.5 1.3 fusion.138
  9.2 3.0 select_bitcast_fusion.1
  12.2 0.0 all-reduce.3.cloned.1.call-update
  12.2 0.2 cosine_multiply_fusion
  12.4 104.8 %all-reduce.3.cloned.1.call-done = (bf16[32,128,128]{2,1,0:T(8,128)(2,1)}, bf16[32,128,128]{2,1,0:T(8,128)(2,1)}) async-done(((bf16[32,128,128]{2,1,0:T(8,128)(2,1)}, bf16[32,128,128]{2,1,0:T(8,128)(2,1)}), (bf16[32,128,128]{2,1,0:T(8,128)(2,1)}, bf16[32,128,128]{2,1,0:T(8,128)(2,1)})) %all-reduce.3.cloned.1.call-update) | async-done | bytes 2097168 | tf_op jit(solution)/shard_map/psum | solution.py:19
  117.2 1.5 convert_element_type.60
  118.6 16.4 %fusion = f32[6,32,128,128]{2,3,1,0:T(8,128)S(1)} fusion(bf16[6,32,128,128]{3,2,1,0:T(8,128)(2,1)} %param.7, f32[32,128,128]{2,1,0:T(8,128)S(1)} %convert_element_type.60, f32[128,64]{0,1:T(8,128)S(1)} %get-tuple-element.14, f32[128,64]{0,1:T(8,128)S(1)} %get-tuple-element.13), kind=kOutput, calls=%fused_computation.3 | convolution fusion | flops 4838146048 | bytes 21037056 | tf_op jit(solution)/shard_map/fxyz,zq->fxyq/dot_general | solution.py:33
  135.1 18.5 %fusion.12 = f32[64,6,32,64]{3,0,2,1:T(8,128)S(1)} fusion(f32[6,32,128,128]{2,3,1,0:T(8,128)S(1)} %fusion, s32[64]{0:T(128)S(1)} %iota_add_fusion), kind=kOutput, calls=%fused_computation.23 | convolution fusion | flops 1208082432 | bytes 9437696 | tf_op jit(solution)/shard_map/fxyk,yq->fxqk/dot_general | solution.py:38
  153.5 18.5 %fusion.14 = f32[64,6,32,64]{3,0,2,1:T(8,128)S(1)} fusion(f32[6,32,128,128]{2,3,1,0:T(8,128)S(1)} %fusion, s32[64]{0:T(128)S(1)} %iota_add_fusion), kind=kOutput, calls=%fused_computation.25 | convolution fusion | flops 1208090624 | bytes 9437696 | tf_op jit(solution)/shard_map/fxyk,yq->fxqk/dot_general | solution.py:35
  172.1 18.8 %add_bitcast_fusion.1 = f32[6,32,64,64]{3,2,1,0:T(8,128)S(1)} fusion(f32[64,6,32,64]{3,0,2,1:T(8,128)S(1)} %fusion.12, f32[6,32,128,128]{2,3,1,0:T(8,128)S(1)} %fusion, s32[64]{0:T(128)S(1)} %iota_add_fusion), kind=kOutput, calls=%fused_computation.12 | convolution fusion | flops 1208877056 | bytes 15729152 | tf_op jit(solution)/shard_map/fxyk,yq->fxqk/dot_general | solution.py:38
  190.8 20.4 %subtract_bitcast_fusion.1 = f32[6,32,64,64]{3,2,1,0:T(8,128)} fusion(f32[64,6,32,64]{3,0,2,1:T(8,128)S(1)} %fusion.14, f32[6,32,128,128]{2,3,1,0:T(8,128)S(1)} %fusion, s32[64]{0:T(128)S(1)} %iota_add_fusion), kind=kOutput, calls=%fused_computation.13 | convolution fusion | flops 1208868864 | bytes 15729152 | tf_op jit(solution)/shard_map/fxyk,yq->fxqk/dot_general | solution.py:35
  211.3 4.5 pad_maximum_fusion
  215.8 6.2 copy.40
  222.0 5.4 all-to-all-start
  227.4 0.0 copy-done.5
  227.4 0.2 convert_element_type.61
  227.6 16.3 %fusion.1 = f32[6,32,128,128]{2,3,1,0:T(8,128)S(1)} fusion(bf16[6,32,128,128]{3,2,1,0:T(8,128)(2,1)} %param.7, f32[32,128,128]{2,1,0:T(8,128)S(1)} %convert_element_type.61, f32[128,64]{0,1:T(8,128)S(1)} %get-tuple-element.14, f32[128,64]{0,1:T(8,128)S(1)} %get-tuple-element.13), kind=kOutput, calls=%fused_computation.4 | convolution fusion | flops 4838146048 | bytes 21037056 | tf_op jit(solution)/shard_map/fxyz,zq->fxyq/dot_general | solution.py:33
  244.0 18.5 %fusion.6 = f32[64,6,32,64]{3,0,2,1:T(8,128)S(1)} fusion(f32[6,32,128,128]{2,3,1,0:T(8,128)S(1)} %fusion.1, s32[64]{0:T(128)S(1)} %iota_add_fusion), kind=kOutput, calls=%fused_computation.17 | convolution fusion | flops 1208090624 | bytes 9437696 | tf_op jit(solution)/shard_map/fxyk,yq->fxqk/dot_general | solution.py:35
  262.5 18.7 %fusion.4 = f32[64,6,32,64]{3,0,2,1:T(8,128)S(1)} fusion(f32[6,32,128,128]{2,3,1,0:T(8,128)S(1)} %fusion.1, s32[64]{0:T(128)S(1)} %iota_add_fusion), kind=kOutput, calls=%fused_computation.15 | convolution fusion | flops 1208082432 | bytes 9437696 | tf_op jit(solution)/shard_map/fxyk,yq->fxqk/dot_general | solution.py:38
  281.2 18.5 %subtract_bitcast_fusion = f32[6,32,64,64]{3,2,1,0:T(8,128)S(1)} fusion(f32[64,6,32,64]{3,0,2,1:T(8,128)S(1)} %fusion.6, f32[6,32,128,128]{2,3,1,0:T(8,128)S(1)} %fusion.1, s32[64]{0:T(128)S(1)} %iota_add_fusion), kind=kOutput, calls=%fused_computation.10 | convolution fusion | flops 1208868864 | bytes 15729152 | tf_op jit(solution)/shard_map/fxyk,yq->fxqk/dot_general | solution.py:35
  299.7 20.3 %add_bitcast_fusion = f32[6,32,64,64]{3,2,1,0:T(8,128)} fusion(f32[64,6,32,64]{3,0,2,1:T(8,128)S(1)} %fusion.4, f32[6,32,128,128]{2,3,1,0:T(8,128)S(1)} %fusion.1, s32[64]{0:T(128)S(1)} %iota_add_fusion), kind=kOutput, calls=%fused_computation.9 | convolution fusion | flops 1208877056 | bytes 15729152 | tf_op jit(solution)/shard_map/fxyk,yq->fxqk/dot_general | solution.py:38
  320.0 4.6 pad_maximum_fusion.1
  324.6 6.3 %copy.45 = f32[6,32,64,128]{3,1,0,2:T(8,128)} copy(f32[6,32,64,128]{3,2,1,0:T(8,128)S(1)} %pad_maximum_fusion.1) | data formatting | bytes 12582912 | tf_op jit(solution)/shard_map/concatenate | solution.py:41
  330.9 0.0 all-to-all-done
  330.9 5.6 all-to-all-start.1
  336.5 0.0 copy-done.7
  336.5 0.0 copy-done.8
  336.5 0.1 subtract_divide_fusion
  336.6 0.1 div.8
  336.7 0.1 broadcast_in_dim.5
  336.7 0.1 mul.230
  336.8 0.0 copy-done.6
  336.9 8.2 %copy.42 = f32[6,4,32,16,128]{4,3,2,1,0:T(8,128)S(1)} copy(f32[6,4,32,16,128]{4,2,0,3,1:T(8,128)} %bitcast.14) | data formatting | bytes 12582912 | tf_op jit(solution)/shard_map/all_to_all | solution.py:64
  345.1 6.8 %fusion.136 = (f32[6,128,16,64]{3,2,1,0:T(8,128)}, f32[6,128,16,64]{3,2,1,0:T(8,128)}) fusion(f32[6,128,16,128]{3,2,1,0:T(8,128)S(1)} %bitcast.104), kind=kLoop, calls=%fused_computation.157 | loop fusion | bytes 12582912 | tf_op jit(solution)/shard_map/slice | solution.py:45
  351.9 4.6 copy.61
  356.5 6.8 %copy.62 = f32[6,128,16,64]{1,3,2,0:T(8,128)} copy(f32[6,128,16,64]{3,2,1,0:T(8,128)} %get-tuple-element.8) | data formatting | bytes 6291456
  363.3 9.3 %fusion.47 = f32[64,6,16,64]{3,0,2,1:T(8,128)S(1)} fusion(f32[6,128,16,64]{1,3,2,0:T(8,128)S(1)} %copy.61, s32[64]{0:T(128)S(1)} %iota_add_fusion), kind=kOutput, calls=%fused_computation.61 | convolution fusion | flops 604102656 | bytes 4718848 | tf_op jit(solution)/shard_map/fxjk,xq->fqjk/dot_general | solution.py:46
  372.6 9.5 %fusion.45 = f32[64,6,16,64]{3,0,2,1:T(8,128)S(1)} fusion(f32[6,128,16,64]{1,3,2,0:T(8,128)S(1)} %copy-done, s32[64]{0:T(128)S(1)} %iota_add_fusion), kind=kOutput, calls=%fused_computation.59 | convolution fusion | flops 604102656 | bytes 4718848 | tf_op jit(solution)/shard_map/fxjk,xq->fqjk/dot_general | solution.py:49
  382.1 10.5 %subtract_bitcast_fusion.3 = bf16[6,64,16,64]{3,1,2,0:T(8,128)(2,1)} fusion(f32[64,6,16,64]{3,0,2,1:T(8,128)S(1)} %fusion.47, f32[6,128,16,64]{1,3,2,0:T(8,128)S(1)} %copy-done, s32[64]{0:T(128)S(1)} %iota_add_fusion), kind=kOutput, calls=%fused_computation.34 | convolution fusion | flops 604897280 | bytes 5505280 | tf_op jit(solution)/shard_map/fxjk,xq->fqjk/dot_general | solution.py:46
  392.6 10.7 %add_bitcast_fusion.3 = bf16[6,64,16,64]{3,1,2,0:T(8,128)(2,1)} fusion(f32[64,6,16,64]{3,0,2,1:T(8,128)S(1)} %fusion.45, f32[6,128,16,64]{1,3,2,0:T(8,128)S(1)} %copy.61, s32[64]{0:T(128)S(1)} %iota_add_fusion), kind=kOutput, calls=%fused_computation.33 | convolution fusion | flops 604897280 | bytes 5505280 | tf_op jit(solution)/shard_map/fxjk,xq->fqjk/dot_general | solution.py:49
  403.3 3.9 all-to-all-done.1
  407.2 8.2 %copy.47 = f32[6,4,32,16,128]{4,3,2,1,0:T(8,128)S(1)} copy(f32[6,4,32,16,128]{4,2,0,3,1:T(8,128)} %bitcast.25) | data formatting | bytes 12582912 | tf_op jit(solution)/shard_map/all_to_all | solution.py:64
  415.4 6.8 %fusion.137 = (f32[6,128,16,64]{3,2,1,0:T(8,128)}, f32[6,128,16,64]{3,2,1,0:T(8,128)}) fusion(f32[6,128,16,128]{3,2,1,0:T(8,128)S(1)} %bitcast.105), kind=kLoop, calls=%fused_computation.158 | loop fusion | bytes 12582912 | tf_op jit(solution)/shard_map/slice | solution.py:45
  422.2 4.9 copy.63
  427.1 11.0 %fusion.41 = f32[64,6,16,64]{3,0,2,1:T(8,128)} fusion(f32[6,128,16,64]{1,3,2,0:T(8,128)S(1)} %copy.63, s32[64]{0:T(128)S(1)} %iota_add_fusion), kind=kOutput, calls=%fused_computation.55 | convolution fusion | flops 604102656 | bytes 4718848 | tf_op jit(solution)/shard_map/fxjk,xq->fqjk/dot_general | solution.py:46
  438.1 6.8 %copy.64 = f32[6,128,16,64]{1,3,2,0:T(8,128)} copy(f32[6,128,16,64]{3,2,1,0:T(8,128)} %get-tuple-element.10) | data formatting | bytes 6291456
  444.9 11.3 %fusion.39 = f32[64,6,16,64]{3,0,2,1:T(8,128)S(1)} fusion(f32[6,128,16,64]{1,3,2,0:T(8,128)} %copy.64, s32[64]{0:T(128)S(1)} %iota_add_fusion), kind=kOutput, calls=%fused_computation.53 | convolution fusion | flops 604102656 | bytes 4718848 | tf_op jit(solution)/shard_map/fxjk,xq->fqjk/dot_general | solution.py:49
  456.3 9.5 %subtract_bitcast_fusion.2 = bf16[6,64,16,64]{3,1,2,0:T(8,128)(2,1)S(1)} fusion(f32[64,6,16,64]{3,0,2,1:T(8,128)S(1)} %copy-done.2, f32[6,128,16,64]{1,3,2,0:T(8,128)S(1)} %copy-done.1, s32[64]{0:T(128)S(1)} %iota_add_fusion), kind=kOutput, calls=%fused_computation.32 | convolution fusion | flops 604897280 | bytes 5505280 | tf_op jit(solution)/shard_map/fxjk,xq->fqjk/dot_general | solution.py:46
  465.8 9.3 %add_bitcast_fusion.2 = bf16[6,64,16,64]{3,1,2,0:T(8,128)(2,1)S(1)} fusion(f32[64,6,16,64]{3,0,2,1:T(8,128)S(1)} %fusion.39, f32[6,128,16,64]{1,3,2,0:T(8,128)S(1)} %copy.63, s32[64]{0:T(128)S(1)} %iota_add_fusion), kind=kOutput, calls=%fused_computation.31 | convolution fusion | flops 604897280 | bytes 5505280 | tf_op jit(solution)/shard_map/fxjk,xq->fqjk/dot_general | solution.py:49
  475.2 2.0 maximum_maximum_fusion
  477.2 5.5 reshape.36
  482.7 10.3 %copy.66 = bf16[12,64,16,2,64]{4,2,1,3,0:T(8,128)(2,1)} copy(bf16[12,64,16,2,64]{4,3,1,2,0:T(2,128)(2,1)} %reshape.36) | data formatting | bytes 6291456 | tf_op jit(solution)/shard_map/reshape | solution.py:70
  493.1 74.7 %copy.60 = bf16[12,2,64,16,64]{0,1,4,3,2:T(2,128)(2,1)} copy(bf16[12,2,64,16,64]{4,3,2,1,0:T(8,128)(2,1)} %bitcast.107) | data formatting | bytes 6291456 | tf_op jit(solution)/shard_map/reshape | solution.py:72
  567.8 9.2 %gather_fusion = bf16[320,12,2]{1,2,0:T(2,128)(2,1)S(1)} fusion(bf16[12,2,65536]{0,1,2:T(2,128)(2,1)} %bitcast.106, s32[1024]{0:T(1024)S(1)} %pad_clamp_fusion), kind=kCustom, calls=%fused_computation | custom fusion | bytes 32000 | tf_op jit(solution)/shard_map/gather | solution.py:74
  577.0 0.1 copy.52
  577.1 5.3 all-gather
  582.4 0.1 reshape.48
  582.6 0.2 all_to_all.48
  582.7 0.7 copy.54
  583.4 4.4 all-to-all-start.2
  587.7 0.1 multiply_convert_fusion
  587.8 31.2 %all_gather.7 = bf16[192,128]{1,0:T(8,128)(2,1)S(1)} all-gather(bf16[24,128]{1,0:T(8,128)(2,1)S(1)} %multiply_convert_fusion), channel_id=1, replica_groups=mesh['band'=8,'ga'=4] {'band'}, dimensions={0}, use_global_device_ids=true | all-gather | bytes 55296 | tf_op jit(solution)/shard_map/all_gather | solution.py:84
  619.0 0.0 all-to-all-done.2
  619.0 0.8 fusion.139
  (20 shorter events, 0.1 us)
Async XLA Ops:
  6.5 110.6 %all-reduce.3.cloned.1.call-start = ((), (), s32[]{:S(2)}) async-start(), calls=%async_computation.3 | async-start | bytes 4194304 | tf_op jit(solution)/shard_map/psum | solution.py:19
  222.0 5.4 copy-start.5
  222.0 108.9 %all-to-all-start = ((f32[6,32,64,128]{3,1,0,2:T(8,128)}), f32[6,32,64,128]{3,1,0,2:T(8,128)}, u32[]{:S(2)}, u32[]{:S(2)}) async-start(f32[6,32,64,128]{3,1,0,2:T(8,128)} %copy.40), calls=%async_computation | async-start | bytes 12582912 | tf_op jit(solution)/shard_map/all_to_all | solution.py:64
  330.9 5.6 copy-start.7
  330.9 5.6 copy-start.8
  330.9 6.0 copy-start.6
  330.9 76.3 %all-to-all-start.1 = ((f32[6,32,64,128]{3,1,0,2:T(8,128)}), f32[6,32,64,128]{3,1,0,2:T(8,128)}, u32[]{:S(2)}, u32[]{:S(2)}) async-start(f32[6,32,64,128]{3,1,0,2:T(8,128)} %copy.45), calls=%async_computation.1 | async-start | bytes 12582912 | tf_op jit(solution)/shard_map/all_to_all | solution.py:64
  363.3 9.3 %copy-start = (f32[6,128,16,64]{1,3,2,0:T(8,128)S(1)}, f32[6,128,16,64]{1,3,2,0:T(8,128)}, u32[]{:S(2)}) copy-start(f32[6,128,16,64]{1,3,2,0:T(8,128)} %copy.62) | copy-start | bytes 9437188
  444.9 11.4 %copy-start.1 = (f32[6,128,16,64]{1,3,2,0:T(8,128)S(1)}, f32[6,128,16,64]{1,3,2,0:T(8,128)}, u32[]{:S(2)}) copy-start(f32[6,128,16,64]{1,3,2,0:T(8,128)} %copy.64) | copy-start | bytes 9437188
  444.9 11.3 %copy-start.2 = (f32[64,6,16,64]{3,0,2,1:T(8,128)S(1)}, f32[64,6,16,64]{3,0,2,1:T(8,128)}, u32[]{:S(2)}) copy-start(f32[64,6,16,64]{3,0,2,1:T(8,128)} %fusion.41) | copy-start | bytes 4718596
  456.3 18.8 %copy-start.3 = (bf16[6,64,16,64]{3,1,2,0:T(8,128)(2,1)S(1)}, bf16[6,64,16,64]{3,1,2,0:T(8,128)(2,1)}, u32[]{:S(2)}) copy-start(bf16[6,64,16,64]{3,1,2,0:T(8,128)(2,1)} %subtract_bitcast_fusion.3) | copy-start | bytes 2359300
  456.3 18.8 %copy-start.4 = (bf16[6,64,16,64]{3,1,2,0:T(8,128)(2,1)S(1)}, bf16[6,64,16,64]{3,1,2,0:T(8,128)(2,1)}, u32[]{:S(2)}) copy-start(bf16[6,64,16,64]{3,1,2,0:T(8,128)(2,1)} %add_bitcast_fusion.3) | copy-start | bytes 2359300
  583.4 35.6 %all-to-all-start.2 = ((bf16[24,8,160]{2,0,1:T(8,128)(2,1)}), bf16[24,8,160]{2,0,1:T(8,128)(2,1)S(1)}, u32[]{:S(2)}, u32[]{:S(2)}) async-start(bf16[24,8,160]{2,0,1:T(8,128)(2,1)} %copy.54), calls=%async_computation.2 | async-start | bytes 196608 | tf_op jit(solution)/shard_map/all_to_all | solution.py:83
Sparse Core Ops, SparseCore 0:
  12.3 104.8 all-reduce.2
where the time goes:
time: 640 us; the launch traced here: 627 us
  matrix products  267 us (42%)
  local copies, waits for them, and re-layouts  168 us (26%)
  waiting for transfers between devices  109 us (17%)
  blocking collectives  36.5 us (6%)
  other arithmetic  16.1 us (3%)
  starting transfers between devices  15.3 us (2%)
  between operations  15.2 us (2%)
    psum x1, waiting for transfers between devices, spread_2(): return lax.psum(block, axis)  105 us
    reshape x1, local copies, waits for them, and re-layouts, per_device(): arranged = spectra.reshape(field_count, KB, kyd_local, 2, KB).transpose(0...  74.7 us
    dot_general x2, matrix products, front_half(): jnp.einsum('fxyk,yq->fxqk', real_z, sine_table, precision=highest)  39.1 us
    dot_general x2, matrix products, front_half(): jnp.einsum('fxyk,yq->fxqk', real_z, cosine_table, precision=highest)  38.9 us
    dot_general x2, matrix products, front_half(): jnp.einsum('fxyk,yq->fxqk', imag_z, cosine_table, precision=highest)  37.2 us
    dot_general x2, matrix products, front_half(): jnp.einsum('fxyk,yq->fxqk', imag_z, sine_table, precision=highest)  37.1 us
    dot_general x2, matrix products, front_half(): zpart = jnp.einsum('fxyz,zq->fxyq', fields, both_tables, precision=highest)  32.8 us
    all_gather x1, blocking collectives, per_device(): panel_all = lax.all_gather(weighted, 'band', axis=0, tiled=True)  31.2 us
  transfers between devices with their start and end apart: 4, of which 2 were waited for; matrix products, arithmetic and copies ran while one was open for 27% of the time, Pallas kernels for 0%

commit v1 on v0

v1 whole, which is shorter than its diff:
```python
import functools
import math

import jax
import jax.numpy as jnp
import numpy as np
from jax import lax
from jax.experimental import pallas as pl
from jax.experimental.pallas import tpu as pltpu
from jax.sharding import PartitionSpec as P

KB = 64
PANEL_DEV = 128
SLOTS = 64
CHUNKS = 4

F32 = jnp.float32
BF16 = jnp.bfloat16


def round_up(value, step):
    return -(-value // step) * step


def tables(grid_count):
    grid_points = np.arange(grid_count)
    freqs = np.arange(KB + 1) - KB // 2
    angles = (grid_points[:, None] * freqs[None, :] % grid_count) * (2.0 * math.pi / grid_count)
    scale = 1.0 / math.sqrt(grid_count)
    return np.cos(angles) * scale, -np.sin(angles) * scale


def split_np(values):
    high = np.asarray(values, np.float32).astype(jnp.bfloat16)
    low = (np.asarray(values, np.float64) - high.astype(np.float64)).astype(jnp.bfloat16)
    return high, low


def split(values):
    high = values.astype(BF16)
    return high, (values - high.astype(F32)).astype(BF16)


def mxu(a, b):
    return jnp.dot(a, b, preferred_element_type=F32)


def spectrum_kernel(
    dims, count_ref, group_ref, cond_ref, val_ref, ty_ref, tz_ref, tx_ref, meta_ref, slot_ref,
    out_ref, real_ref, imag_ref,
):
    n_val, n_cond, planes, grid_count, half_pad, stride = dims
    band = pl.program_id(0)
    field_rows = n_val * n_cond * planes

    def one_plane(x, carry):
        wave = cond_ref[0, x].astype(F32)
        pairs = [split(wave * val_ref[k, x].astype(F32)) for k in range(n_val)]
        stacked = jnp.concatenate(
            [
                jnp.concatenate([p[0] for p in pairs], axis=1),
                jnp.concatenate([p[1] for p in pairs], axis=1),
            ],
            axis=0,
        )
        both = mxu(ty_ref[...], stacked)
        both = both[: 2 * half_pad] + both[2 * half_pad :]
        for k in range(n_val):
            row = (k * n_cond + band) * planes + x
            cols = slice(k * grid_count, (k + 1) * grid_count)
            real_ref[pl.ds(row, half_pad, stride=stride), :] = both[:half_pad, cols]
            imag_ref[pl.ds(row, half_pad, stride=stride), :] = both[half_pad:, cols]
        return carry

    lax.fori_loop(0, planes, one_plane, 0, unroll=2)

    @pl.when(band == n_cond - 1)
    def _():
        out_ref[...] = jnp.zeros_like(out_ref)
        lane = lax.broadcasted_iota(jnp.int32, (1, 2 * SLOTS), 1)
        sign = jnp.where(lane < SLOTS, -1.0, 1.0).astype(F32)

        def one_tile(t, carry):
            start = pl.multiple_of(group_ref[t] * stride, 8)
            half = jnp.concatenate(
                [real_ref[pl.ds(start, field_rows), :], imag_ref[pl.ds(start, field_rows), :]], axis=1
            )
            high, low = split(half)
            meta = meta_ref[t]
            pick_z = (lax.broadcasted_iota(jnp.int32, (2 * KB, 2 * SLOTS), 0) == meta[0:1]).astype(F32).astype(BF16)
            turn = meta[2:3].astype(F32)
            basis_high = mxu(tz_ref[0], pick_z)
            basis_low = mxu(tz_ref[1], pick_z)

            def conjugated(basis):
                return jnp.concatenate([basis[:grid_count], basis[grid_count:] * turn], axis=0).astype(BF16)

            basis_high, basis_low = conjugated(basis_high), conjugated(basis_low)
            wide = mxu(high, jnp.concatenate([basis_high, basis_low], axis=1))
            at_g = wide[:, : 2 * SLOTS] + wide[:, 2 * SLOTS :] + mxu(low, basis_high)
            pick_x = (lax.broadcasted_iota(jnp.int32, (KB, 2 * SLOTS), 0) == meta[1:2]).astype(F32).astype(BF16)
            phase = mxu(tx_ref[...], jnp.concatenate([pick_x, pick_x], axis=0))
            rows = phase.shape[0] // 2
            cosine, sine = phase[:rows], phase[rows:] * sign
            turned = pltpu.roll(at_g, SLOTS, axis=1)
            if rows == field_rows:
                moved = at_g * cosine + turned * sine
                field = lax.broadcasted_iota(jnp.int32, (n_val * n_cond, field_rows), 0)
                owner = lax.broadcasted_iota(jnp.int32, (n_val * n_cond, field_rows), 1) // planes
                adder = (field == owner).astype(F32).astype(BF16)
                moved_high, moved_low = split(moved)
                summed = mxu(adder, moved_high) + mxu(adder, moved_low)
            else:
                shape = (n_val * n_cond, planes, 2 * SLOTS)
                moved = at_g.reshape(shape) * cosine[None] + turned.reshape(shape) * sine[None]
                summed = jnp.sum(moved, axis=1)
            n_fields = n_val * n_cond
            fields_pad = out_ref.shape[0] // 2
            summed = jnp.concatenate(
                [summed, jnp.zeros((fields_pad - n_fields, 2 * SLOTS), F32)], axis=0
            )
            parts = jnp.concatenate(
                [summed[:, :SLOTS], pltpu.roll(summed, SLOTS, axis=1)[:, :SLOTS]], axis=0
            )
            parts_high, parts_low = split(parts)
            place = lax.broadcasted_iota(jnp.int32, (SLOTS, slot_ref.shape[1]), 0) + t * SLOTS
            back = (place == slot_ref[...]).astype(F32).astype(BF16)
            placed = mxu(jnp.concatenate([parts_high, parts_low], axis=0), back)
            out_ref[...] += placed[: 2 * fields_pad] + placed[2 * fields_pad :]
            return carry

        lax.fori_loop(0, count_ref[0], one_tile, 0)


def plan_slots(gvec_all, per_block, n_ga):
    n_g = gvec_all.shape[0]
    kyd = KB // n_ga
    n_groups = KB // 2 + 1
    n_tiles = n_groups + -(-n_g // SLOTS)
    block = jnp.arange(n_g, dtype=jnp.int32) // per_block
    q_x = gvec_all // (kyd * KB)
    freq_y = block * kyd + gvec_all // KB % kyd - KB // 2
    q_z = gvec_all % KB
    group = jnp.abs(freq_y)
    member = (jnp.arange(n_groups, dtype=jnp.int32)[:, None] == group[None, :]).astype(jnp.int32)
    counts = jnp.sum(member, axis=1)
    group_tiles = (counts + SLOTS - 1) // SLOTS
    before = jnp.arange(n_groups)[:, None] > jnp.arange(n_groups)[None, :]
    first_tile = jnp.sum(jnp.where(before, group_tiles[None, :], 0), axis=1)
    index = jnp.arange(n_g, dtype=jnp.int32)
    earlier = (group[:, None] == group[None, :]) & (index[:, None] > index[None, :])
    rank = jnp.sum(earlier.astype(jnp.int32), axis=1)
    slot = jnp.sum(member * first_tile[:, None], axis=0) * SLOTS + rank
    packed = (q_x * KB + q_z) * 2 + (freq_y < 0).astype(jnp.int32)
    slots = jnp.arange(n_tiles * SLOTS, dtype=jnp.int32)
    by_slot = jnp.sum(jnp.where(slots[:, None] == slot[None, :], packed[None, :], 0), axis=1)
    by_slot = by_slot.reshape(n_tiles, SLOTS)
    slot_z = by_slot // 2 % KB
    slot_x = by_slot // 2 // KB
    turn = 1 - 2 * (by_slot % 2)
    rows = [
        jnp.concatenate([slot_z, slot_z + KB], axis=1),
        jnp.concatenate([slot_x, slot_x], axis=1),
        jnp.concatenate([turn, turn], axis=1),
    ]
    meta = jnp.stack(rows + [jnp.zeros_like(rows[0])] * 5, axis=1)
    last_tile = first_tile + group_tiles
    tiles = jnp.arange(n_tiles, dtype=jnp.int32)
    tile_group = jnp.sum((last_tile[None, :] <= tiles[:, None]).astype(jnp.int32), axis=1)
    tile_group = jnp.minimum(tile_group, n_groups - 1)
    return jnp.sum(group_tiles).reshape(1), tile_group, meta, slot.reshape(1, n_g)


def gather_blocks(block, n_ga):
    held, hop = block[None], 1
    while hop < n_ga:
        other = lax.ppermute(held, "ga", [(i, i ^ hop) for i in range(n_ga)])
        held = jnp.concatenate([held, other], axis=0)
        hop *= 2
    me, hop = lax.axis_index("ga"), 1
    while hop < n_ga:
        pairs = held.reshape(-1, 2, hop, block.shape[0])
        held = jnp.where(me // hop % 2 == 1, pairs[:, ::-1], pairs)
        hop *= 2
    return held.reshape(-1)


def spread_bands(local, owners, n_band):
    n_val, planes, height, width = local.shape
    me = lax.axis_index("band")
    ring = list(range(0, n_band, 2)) + list(range(n_band - 1, 0, -2))
    place = np.zeros(n_band, np.int32)
    for spot, device in enumerate(ring):
        place[device] = spot
    place = jnp.asarray(place)
    ahead = [(ring[i], ring[(i + 1) % n_band]) for i in range(n_band)]
    behind = [(b, a) for a, b in ahead]
    rows = planes * height
    chunk = rows // (2 * CHUNKS)
    flat = local.reshape(n_val, 2, CHUNKS, chunk, width)
    bands = []
    for k in range(n_val):
        is_root = me == owners[k]
        distance = (place[me] - place[owners[k]]) % n_band
        halves = []
        for way, perm in enumerate((ahead, behind)):
            held, received = None, []
            for step in range(CHUNKS + n_band - 2):
                if held is None:
                    send = flat[k, way, 0]
                elif step < CHUNKS:
                    send = jnp.where(is_root, flat[k, way, step], held)
                else:
                    send = held
                held = lax.ppermute(send, "band", perm)
                received.append(held)
            hops = distance if way == 0 else (n_band - distance) % n_band
            start = jnp.maximum(hops - 1, 0)
            arrived = lax.dynamic_slice_in_dim(jnp.stack(received), start, CHUNKS, 0)
            halves.append(jnp.where(is_root, flat[k, way], arrived))
        bands.append(jnp.stack(halves).reshape(planes, height, width))
    return jnp.stack(bands)


def per_device(valence, conduction, owners, val_energy, cond_energy, gvec_index, *, n_band, n_ga):
    local_val = valence[0]
    n_val = local_val.shape[0]
    n_cond, planes, grid_count, _ = conduction.shape
    n_fields = n_val * n_cond
    field_rows = n_fields * planes
    per_block = gvec_index.shape[0]
    n_g = per_block * n_ga
    half = KB // 2

    gvec_all = gather_blocks(gvec_index, n_ga)
    count, tile_group, meta, slot = plan_slots(gvec_all, per_block, n_ga)
    fields = spread_bands(local_val, owners, n_band)

    cosine, sine = tables(grid_count)
    half_pad = round_up(half + 1, 8)
    stride = round_up(field_rows, 8)
    stride += 8 * (1 - stride // 8 % 2)
    ty = np.zeros((2 * half_pad, grid_count))
    ty[: half + 1] = cosine[:, half:].T
    ty[half_pad : half_pad + half + 1] = sine[:, half:].T
    ty_high, ty_low = split_np(ty)
    ty = np.concatenate([np.tile(ty_high, (1, 2)), np.tile(ty_low, (1, 2))], axis=0)
    cos_z, sin_z = cosine[:, :KB], sine[:, :KB]
    tz = np.stack(split_np(np.block([[cos_z, sin_z], [-sin_z, cos_z]])))
    cos_x = np.concatenate(split_np(cos_z), axis=1)
    sin_x = np.concatenate(split_np(sin_z), axis=1)
    start = lax.axis_index("ga") * planes
    tx = [lax.dynamic_slice_in_dim(jnp.asarray(part), start, planes, 0) for part in (cos_x, sin_x)]
    if planes % 8:
        tx = [jnp.tile(part, (n_fields, 1)) for part in tx]
    tx = jnp.concatenate(tx, axis=0)

    fields_pad = round_up(n_fields, 8)
    whole = lambda shape: pl.BlockSpec(shape, lambda i, *_: (0,) * len(shape))
    partial_sums = pl.pallas_call(
        functools.partial(spectrum_kernel, (n_val, n_cond, planes, grid_count, half_pad, stride)),
        out_shape=jax.ShapeDtypeStruct((2 * fields_pad, n_g), F32),
        grid_spec=pltpu.PrefetchScalarGridSpec(
            num_scalar_prefetch=2,
            grid=(n_cond,),
            in_specs=[
                pl.BlockSpec((1, planes, grid_count, grid_count), lambda i, *_: (i, 0, 0, 0)),
                whole(fields.shape),
                whole(ty.shape),
                whole(tz.shape),
                whole(tx.shape),
                whole(meta.shape),
                whole(slot.shape),
            ],
            out_specs=whole((2 * fields_pad, n_g)),
            scratch_shapes=[pltpu.VMEM((half_pad * stride, grid_count), F32)] * 2,
        ),
        compiler_params=pltpu.CompilerParams(vmem_limit_bytes=48 * 1024 * 1024),
    )(count, tile_group, conduction, fields, jnp.asarray(ty), jnp.asarray(tz), tx, meta, slot)

    total = partial_sums.reshape(2, fields_pad, n_g)[:, :n_fields].reshape(2 * n_fields, n_g)
    hop = 1
    while hop < n_ga:
        total = total + lax.ppermute(total, "ga", [(i, i ^ hop) for i in range(n_ga)])
        hop *= 2
    coeffs = total.astype(BF16)
    weights = 1.0 / (val_energy[:, None] - cond_energy[None, :])
    row_weights = jnp.tile(weights.reshape(-1), 2)
    panel = lax.dynamic_slice_in_dim(coeffs, lax.axis_index("ga") * per_block, PANEL_DEV, 1)
    weighted = (panel.astype(F32) * row_weights[:, None]).astype(BF16)
    rows_per = n_g // n_band
    by_band = coeffs.reshape(2 * n_fields, n_band, rows_per).transpose(1, 0, 2)
    sent = jnp.concatenate(
        [by_band, jnp.broadcast_to(weighted[None], (n_band,) + weighted.shape)], axis=2
    )
    arrived = lax.all_to_all(sent, "band", split_axis=0, concat_axis=0, tiled=True)
    arrived = arrived.reshape(n_band * 2 * n_fields, rows_per + PANEL_DEV)
    return lax.dot_general(
        arrived[:, :rows_per], arrived[:, rows_per:], (((0,), (0,)), ((), ())), preferred_element_type=F32
    )


def solution(mesh):
    in_specs = (
        P("band", None, "ga", None, None),
        P("band", "ga", None, None),
        P(),
        P(),
        P("band"),
        P("ga"),
    )
    body = functools.partial(per_device, n_band=mesh.shape["band"], n_ga=mesh.shape["ga"])
    return jax.shard_map(body, mesh=mesh, in_specs=in_specs, out_specs=P("band", "ga"), check_vma=False)
```

time: 640 us -> 163 us (0.25); the launches traced: 627 us -> 163 us
  matrix products: 267 us -> 0.88 us
  local copies, waits for them, and re-layouts: 168 us -> 9.81 us
  waiting for transfers between devices: 109 us -> 31.9 us
  Pallas kernels: 0 us -> 48.4 us
  starting transfers between devices: 15.3 us -> 46.1 us
  blocking collectives: 36.5 us -> 11.4 us
  other arithmetic: 16.1 us -> 6.21 us
  between operations: 15.2 us -> 8.17 us
    dot_general x19 -> x1, matrix products: 267 us -> 0.88 us  [per_device(): lax.dot_general(arrived[:, :rows_per], arrived[:, rows_per:], (((0,), (0,...]
    psum x1 -> x0, waiting for transfers between devices: 105 us -> none  [spread_2(): return lax.psum(block, axis)]
    reshape x3 -> x6, local copies, waits for them, and re-layouts: 90.6 us -> 0.36 us  [the longest x2 0.18 us: per_device(): by_band = coeffs.reshape(2 * n_fields, n_band, rows_per).transpose(1, 0, 2)]
    pallas_call x0 -> x1, Pallas kernels: none -> 48.4 us  [per_device(): pl.pallas_call(functools.partial(spectrum_kernel, (n_val, n_cond, planes,...]
    ppermute x0 -> x44, starting transfers between devices: none -> 46.1 us  [the longest x40 42.6 us: spread_bands(): held = lax.ppermute(send, 'band', perm)]
    all_gather x2 -> x0, blocking collectives: 36.5 us -> none  [the longest x1 31.2 us: per_device(): panel_all = lax.all_gather(weighted, 'band', axis=0, tiled=True)]
    ppermute x0 -> x44, waiting for transfers between devices: none -> 31.9 us  [the longest x40 25.2 us: spread_bands(): held = lax.ppermute(send, 'band', perm)]
    unnamed x23 -> x46, local copies, waits for them, and re-layouts: 23.3 us -> 1.38 us
  transfers between devices with their start and end apart: 4 -> 44, of which waited for: 2 -> 30; matrix products, arithmetic and copies ran while one was open for 27% -> 8% of each run, Pallas kernels for 0% -> 0%
where the time goes in v1:
time: 163 us
  Pallas kernels  48.4 us (30%)
  starting transfers between devices  46.1 us (28%)
  waiting for transfers between devices  31.9 us (20%)
  blocking collectives  11.4 us (7%)
  local copies, waits for them, and re-layouts  9.81 us (6%)
  between operations  8.17 us (5%)
  other arithmetic  6.21 us (4%)
    pallas_call x1, Pallas kernels, per_device(): pl.pallas_call(functools.partial(spectrum_kernel, (n_val, n_cond, planes,...  48.4 us
    ppermute x40, starting transfers between devices, spread_bands(): held = lax.ppermute(send, 'band', perm)  42.6 us
    ppermute x40, waiting for transfers between devices, spread_bands(): held = lax.ppermute(send, 'band', perm)  25.2 us
    all_to_all x1, blocking collectives, per_device(): lax.all_to_all(sent, 'band', split_axis=0, concat_axis=0, tiled=True)  11.4 us
    ppermute x2, waiting for transfers between devices, per_device(): lax.ppermute(total, 'ga', [(i, i ^ hop) for i in range(n_ga)])  4.96 us
  transfers between devices with their start and end apart: 44, of which 30 were waited for; matrix products, arithmetic and copies ran while one was open for 8% of the time, Pallas kernels for 0%

profile of v1, /device:TPU:0, one launch (start us, length us, event | category | flops | bytes accessed | tf_op | source)
XLA Modules:
  0.0 162.9 jit_solution(16910236419789568359)
XLA Ops:
  0.0 1.3 slice_bitcast_fusion.19
  1.3 3.0 %collective-permute-start.12 = (bf16[512,128]{1,0:T(8,128)(2,1)S(1)}, bf16[512,128]{1,0:T(8,128)(2,1)S(1)}, u32[]{:S(2)}, u32[]{:S(2)}) collective-permute-start(bf16[512,128]{1,0:T(8,128)(2,1)S(1)} %get-tuple-element.28), channel_id=1, source_target_pairs={{8,0},{16,8},{24,16},{28,24},{20,28},{12,20},{4,12},{0,4},{9,1},{1... | collective-permute-start | bytes 393224 | tf_op jit(solution)/shard_map/ppermute | solution.py:215
  4.4 2.0 %collective-permute-start.22 = (bf16[512,128]{1,0:T(8,128)(2,1)S(1)}, bf16[512,128]{1,0:T(8,128)(2,1)S(1)}, u32[]{:S(2)}, u32[]{:S(2)}) collective-permute-start(bf16[512,128]{1,0:T(8,128)(2,1)S(1)} %get-tuple-element.27), channel_id=1, source_target_pairs={{0,8},{8,16},{16,24},{24,28},{28,20},{20,12},{12,4},{4,0},{1,9},{9... | collective-permute-start | bytes 393224 | tf_op jit(solution)/shard_map/ppermute | solution.py:215
  6.5 0.7 broadcast_in_dim.24
  7.1 1.3 fusion.49
  13.6 1.4 fusion.48
  16.3 0.7 constant_dynamic-slice_fusion
  18.3 1.9 %collective-permute-start.1 = (s32[2,320]{1,0:T(2,128)S(1)}, s32[2,320]{1,0:T(2,128)S(1)}, u32[]{:S(2)}, u32[]{:S(2)}) collective-permute-start(s32[2,320]{1,0:T(2,128)S(1)} %pad_add_fusion.2), channel_id=1, source_target_pairs={{0,2},{1,3},{2,0},{3,1},{4,6},{5,7},{6,4},{7,5},{8,10},{9,11},{10,... | collective-permute-start | bytes 7688 | tf_op jit(solution)/shard_map/ppermute | solution.py:177
  20.2 1.7 %collective-permute-done.1 = s32[2,320]{1,0:T(2,128)S(1)} collective-permute-done((s32[2,320]{1,0:T(2,128)S(1)}, s32[2,320]{1,0:T(2,128)S(1)}, u32[]{:S(2)}, u32[]{:S(2)}) %collective-permute-start.1) | collective-permute-done | bytes 2592 | tf_op jit(solution)/shard_map/ppermute | solution.py:177
  22.4 0.7 convert_reduce_fusion
  23.1 0.7 fusion.47
  24.0 1.8 %select_reduce_fusion = s32[3392]{0:T(1024)S(1)} fusion(s32[1280]{0:T(1024)S(1)} %get-tuple-element.33, s32[1280]{0:T(1024)S(1)} %multiply_add_fusion), kind=kLoop, calls=%fused_computation | loop fusion | flops 13021888 | bytes 23808 | tf_op jit(solution)/shard_map/reduce_sum | solution.py:156
  26.2 0.6 stack.221
  26.9 0.6 convert_reduce_fusion.2
  27.5 0.6 stack_broadcast_in_dim.3
  28.1 1.0 stack.223.meta_ref
  29.1 0.6 broadcast_minimum_fusion.group_ref
  29.8 2.0 %collective-permute-start.13 = (bf16[512,128]{1,0:T(8,128)(2,1)S(1)}, bf16[512,128]{1,0:T(8,128)(2,1)S(1)}, u32[]{:S(2)}, u32[]{:S(2)}) collective-permute-start(bf16[512,128]{1,0:T(8,128)(2,1)S(1)} %get-tuple-element.24), channel_id=1, source_target_pairs={{8,0},{16,8},{24,16},{28,24},{20,28},{12,20},{4,12},{0,4},{9,1},{1... | collective-permute-start | bytes 393224 | tf_op jit(solution)/shard_map/ppermute | solution.py:215
  31.9 2.0 %collective-permute-start.3 = (bf16[512,128]{1,0:T(8,128)(2,1)S(1)}, bf16[512,128]{1,0:T(8,128)(2,1)S(1)}, u32[]{:S(2)}, u32[]{:S(2)}) collective-permute-start(bf16[512,128]{1,0:T(8,128)(2,1)S(1)} %get-tuple-element.21), channel_id=1, source_target_pairs={{0,8},{8,16},{16,24},{24,28},{28,20},{20,12},{12,4},{4,0},{1,9},{9... | collective-permute-start | bytes 393224 | tf_op jit(solution)/shard_map/ppermute | solution.py:215
  34.0 1.7 %collective-permute-done.13 = bf16[512,128]{1,0:T(8,128)(2,1)S(1)} collective-permute-done((bf16[512,128]{1,0:T(8,128)(2,1)S(1)}, bf16[512,128]{1,0:T(8,128)(2,1)S(1)}, u32[]{:S(2)}, u32[]{:S(2)}) %collective-permute-start.13) | collective-permute-done | bytes 131104 | tf_op jit(solution)/shard_map/ppermute | solution.py:215
  35.6 2.0 %collective-permute-done.23 = bf16[512,128]{1,0:T(8,128)(2,1)S(1)} collective-permute-done((bf16[512,128]{1,0:T(8,128)(2,1)S(1)}, bf16[512,128]{1,0:T(8,128)(2,1)S(1)}, u32[]{:S(2)}, u32[]{:S(2)}) %collective-permute-start.23) | collective-permute-done | bytes 131104 | tf_op jit(solution)/shard_map/ppermute | solution.py:215
  37.6 1.4 collective-permute-done.3
  39.1 1.6 collective-permute-start.14
  41.2 1.6 collective-permute-start.34
  43.3 0.9 collective-permute-done.14
  44.2 1.5 collective-permute-done.24
  46.2 1.6 collective-permute-done.4
  47.8 1.6 %collective-permute-start.15 = (bf16[512,128]{1,0:T(8,128)(2,1)S(1)}, bf16[512,128]{1,0:T(8,128)(2,1)S(1)}, u32[]{:S(2)}, u32[]{:S(2)}) collective-permute-start(bf16[512,128]{1,0:T(8,128)(2,1)S(1)} %get-tuple-element.16), channel_id=1, source_target_pairs={{8,0},{16,8},{24,16},{28,24},{20,28},{12,20},{4,12},{0,4},{9,1},{1... | collective-permute-start | bytes 393224 | tf_op jit(solution)/shard_map/ppermute | solution.py:215
  49.9 1.6 collective-permute-start.35
  52.0 2.2 %collective-permute-done.15 = bf16[512,128]{1,0:T(8,128)(2,1)S(1)} collective-permute-done((bf16[512,128]{1,0:T(8,128)(2,1)S(1)}, bf16[512,128]{1,0:T(8,128)(2,1)S(1)}, u32[]{:S(2)}, u32[]{:S(2)}) %collective-permute-start.15) | collective-permute-done | bytes 131104 | tf_op jit(solution)/shard_map/ppermute | solution.py:215
  54.2 1.6 collective-permute-start.16
  56.3 0.7 collective-permute-done.35
  57.0 1.6 collective-permute-start.36
  59.1 0.8 collective-permute-done.16
  59.9 1.6 collective-permute-start.17
  62.4 1.0 collective-permute-done.36
  63.4 1.6 collective-permute-start.37
  65.6 0.7 collective-permute-done.17
  66.3 1.6 collective-permute-start.18
  68.4 0.8 collective-permute-done.37
  69.2 1.6 collective-permute-start.38
  70.8 0.8 collective-permute-start.8
  71.6 1.0 collective-permute-done.18
  72.7 1.6 collective-permute-start.19
  74.8 0.8 collective-permute-done.38
  75.6 1.6 collective-permute-start.39
  77.2 0.6 collective-permute-start.9
  77.8 1.2 collective-permute-done.19
  79.0 1.6 collective-permute-start.20
  81.2 0.7 collective-permute-done.39
  81.8 1.6 collective-permute-start.40
  84.0 1.6 collective-permute-start.21
  86.2 0.6 collective-permute-done.40
  86.8 1.6 collective-permute-start.41
  89.0 1.6 %collective-permute-done.31 = bf16[512,128]{1,0:T(8,128)(2,1)S(1)} collective-permute-done((bf16[512,128]{1,0:T(8,128)(2,1)S(1)}, bf16[512,128]{1,0:T(8,128)(2,1)S(1)}, u32[]{:S(2)}, u32[]{:S(2)}) %collective-permute-start.31) | collective-permute-done | bytes 131104 | tf_op jit(solution)/shard_map/ppermute | solution.py:215
  90.7 1.1 collective-permute-done.41
  91.8 1.6 %collective-permute-done.11 = bf16[512,128]{1,0:T(8,128)(2,1)S(1)} collective-permute-done((bf16[512,128]{1,0:T(8,128)(2,1)S(1)}, bf16[512,128]{1,0:T(8,128)(2,1)S(1)}, u32[]{:S(2)}, u32[]{:S(2)}) %collective-permute-start.11) | collective-permute-done | bytes 131104 | tf_op jit(solution)/shard_map/ppermute | solution.py:215
  94.2 0.7 copy-done
  94.9 48.4 %shard_map.109 = f32[32,1280]{1,0:T(8,128)S(1)} custom-call(s32[1]{0:T(128)} %bitcast.1.count_ref, s32[53]{0:T(128)S(1)} %broadcast_minimum_fusion.group_ref, bf16[6,32,128,128]{3,2,1,0:T(8,128)(2,1)} %cond_ref.1, bf16[2,32,128,128]{3,2,1,0:T(8,128)(2,1)S(1)} %pad_maximum_fusion.val_ref, bf16[160,256]{1,0:T(8,128)(2,1)S(1)} %copy-done.1, ...), custom_call_target="tpu_custom_call" | custom-call | tf_op jit(solution)/shard_map/pallas_call | solution.py:260
  143.4 1.3 collective-permute-done.42
  144.8 1.6 collective-permute-start.43
  146.6 3.6 %collective-permute-done.43 = f32[24,1280]{1,0:T(8,128)S(1)} collective-permute-done((f32[24,1280]{1,0:T(8,128)S(1)}, f32[24,1280]{1,0:T(8,128)S(1)}, u32[]{:S(2)}, u32[]{:S(2)}) %collective-permute-start.43) | collective-permute-done | bytes 122912 | tf_op jit(solution)/shard_map/ppermute | solution.py:284
  150.6 11.4 %all_to_all.5 = bf16[8,24,288]{2,1,0:T(8,128)(2,1)S(1)} all-to-all(bf16[8,24,288]{2,1,0:T(8,128)(2,1)S(1)} %pad_maximum_fusion.3), channel_id=1, replica_groups=mesh['band'=8,'ga'=4] {'band'}, dimensions={0} | all-to-all | bytes 221184 | tf_op jit(solution)/shard_map/all_to_all | solution.py:296
  162.1 0.9 fusion.21
  (130 shorter events, 11.5 us)
Async XLA Ops:
  0.0 29.7 %copy-start.2 = (bf16[1,2,32,128,128]{4,3,2,1,0:T(8,128)(2,1)S(1)}, bf16[1,2,32,128,128]{4,3,2,1,0:T(8,128)(2,1)}, u32[]{:S(2)}) copy-start(bf16[1,2,32,128,128]{4,3,2,1,0:T(8,128)(2,1)} %param.11) | copy-start | bytes 6291460
  1.3 28.4 %collective-permute-start.12 = (bf16[512,128]{1,0:T(8,128)(2,1)S(1)}, bf16[512,128]{1,0:T(8,128)(2,1)S(1)}, u32[]{:S(2)}, u32[]{:S(2)}) collective-permute-start(bf16[512,128]{1,0:T(8,128)(2,1)S(1)} %get-tuple-element.28), channel_id=1, source_target_pairs={{8,0},{16,8},{24,16},{28,24},{20,28},{12,20},{4,12},{0,4},{9,1},{1... | collective-permute-start | bytes 393224 | tf_op jit(solution)/shard_map/ppermute | solution.py:215
  4.3 25.4 %collective-permute-start.2 = (bf16[512,128]{1,0:T(8,128)(2,1)S(1)}, bf16[512,128]{1,0:T(8,128)(2,1)S(1)}, u32[]{:S(2)}, u32[]{:S(2)}) collective-permute-start(bf16[512,128]{1,0:T(8,128)(2,1)S(1)} %get-tuple-element.25), channel_id=1, source_target_pairs={{0,8},{8,16},{16,24},{24,28},{28,20},{20,12},{12,4},{4,0},{1,9},{9... | collective-permute-start | bytes 393224 | tf_op jit(solution)/shard_map/ppermute | solution.py:215
  4.4 25.3 %collective-permute-start.22 = (bf16[512,128]{1,0:T(8,128)(2,1)S(1)}, bf16[512,128]{1,0:T(8,128)(2,1)S(1)}, u32[]{:S(2)}, u32[]{:S(2)}) collective-permute-start(bf16[512,128]{1,0:T(8,128)(2,1)S(1)} %get-tuple-element.27), channel_id=1, source_target_pairs={{0,8},{8,16},{16,24},{24,28},{28,20},{20,12},{12,4},{4,0},{1,9},{9... | collective-permute-start | bytes 393224 | tf_op jit(solution)/shard_map/ppermute | solution.py:215
  6.4 23.3 %collective-permute-start.32 = (bf16[512,128]{1,0:T(8,128)(2,1)S(1)}, bf16[512,128]{1,0:T(8,128)(2,1)S(1)}, u32[]{:S(2)}, u32[]{:S(2)}) collective-permute-start(bf16[512,128]{1,0:T(8,128)(2,1)S(1)} %get-tuple-element.26), channel_id=1, source_target_pairs={{8,0},{16,8},{24,16},{28,24},{20,28},{12,20},{4,12},{0,4},{9,1},{1... | collective-permute-start | bytes 393224 | tf_op jit(solution)/shard_map/ppermute | solution.py:215
  7.1 11.1 %collective-permute-start = (s32[1,320]{1,0:T(1,128)S(1)}, s32[1,320]{1,0:T(1,128)S(1)}, u32[]{:S(2)}, u32[]{:S(2)}) collective-permute-start(s32[1,320]{1,0:T(1,128)S(1)} %broadcast_in_dim.24), channel_id=1, source_target_pairs={{0,1},{1,0},{2,3},{3,2},{4,5},{5,4},{6,7},{7,6},{8,9},{9,8},{10,11... | collective-permute-start | bytes 3848 | tf_op jit(solution)/shard_map/ppermute | solution.py:177
  18.3 3.7 %collective-permute-start.1 = (s32[2,320]{1,0:T(2,128)S(1)}, s32[2,320]{1,0:T(2,128)S(1)}, u32[]{:S(2)}, u32[]{:S(2)}) collective-permute-start(s32[2,320]{1,0:T(2,128)S(1)} %pad_add_fusion.2), channel_id=1, source_target_pairs={{0,2},{1,3},{2,0},{3,1},{4,6},{5,7},{6,4},{7,5},{8,10},{9,11},{10,... | collective-permute-start | bytes 7688 | tf_op jit(solution)/shard_map/ppermute | solution.py:177
  29.8 5.8 %collective-permute-start.13 = (bf16[512,128]{1,0:T(8,128)(2,1)S(1)}, bf16[512,128]{1,0:T(8,128)(2,1)S(1)}, u32[]{:S(2)}, u32[]{:S(2)}) collective-permute-start(bf16[512,128]{1,0:T(8,128)(2,1)S(1)} %get-tuple-element.24), channel_id=1, source_target_pairs={{8,0},{16,8},{24,16},{28,24},{20,28},{12,20},{4,12},{0,4},{9,1},{1... | collective-permute-start | bytes 393224 | tf_op jit(solution)/shard_map/ppermute | solution.py:215
  31.8 5.9 %collective-permute-start.23 = (bf16[512,128]{1,0:T(8,128)(2,1)S(1)}, bf16[512,128]{1,0:T(8,128)(2,1)S(1)}, u32[]{:S(2)}, u32[]{:S(2)}) collective-permute-start(bf16[512,128]{1,0:T(8,128)(2,1)S(1)} %get-tuple-element.23), channel_id=1, source_target_pairs={{0,8},{8,16},{16,24},{24,28},{28,20},{20,12},{12,4},{4,0},{1,9},{9... | collective-permute-start | bytes 393224 | tf_op jit(solution)/shard_map/ppermute | solution.py:215
  31.9 7.2 %collective-permute-start.3 = (bf16[512,128]{1,0:T(8,128)(2,1)S(1)}, bf16[512,128]{1,0:T(8,128)(2,1)S(1)}, u32[]{:S(2)}, u32[]{:S(2)}) collective-permute-start(bf16[512,128]{1,0:T(8,128)(2,1)S(1)} %get-tuple-element.21), channel_id=1, source_target_pairs={{0,8},{8,16},{16,24},{24,28},{28,20},{20,12},{12,4},{4,0},{1,9},{9... | collective-permute-start | bytes 393224 | tf_op jit(solution)/shard_map/ppermute | solution.py:215
  33.8 5.2 %collective-permute-start.33 = (bf16[512,128]{1,0:T(8,128)(2,1)S(1)}, bf16[512,128]{1,0:T(8,128)(2,1)S(1)}, u32[]{:S(2)}, u32[]{:S(2)}) collective-permute-start(bf16[512,128]{1,0:T(8,128)(2,1)S(1)} %get-tuple-element.22), channel_id=1, source_target_pairs={{8,0},{16,8},{24,16},{28,24},{20,28},{12,20},{4,12},{0,4},{9,1},{1... | collective-permute-start | bytes 393224 | tf_op jit(solution)/shard_map/ppermute | solution.py:215
  39.1 5.1 %collective-permute-start.14 = (bf16[512,128]{1,0:T(8,128)(2,1)S(1)}, bf16[512,128]{1,0:T(8,128)(2,1)S(1)}, u32[]{:S(2)}, u32[]{:S(2)}) collective-permute-start(bf16[512,128]{1,0:T(8,128)(2,1)S(1)} %get-tuple-element.20), channel_id=1, source_target_pairs={{8,0},{16,8},{24,16},{28,24},{20,28},{12,20},{4,12},{0,4},{9,1},{1... | collective-permute-start | bytes 393224 | tf_op jit(solution)/shard_map/ppermute | solution.py:215
  40.7 5.0 %collective-permute-start.24 = (bf16[512,128]{1,0:T(8,128)(2,1)S(1)}, bf16[512,128]{1,0:T(8,128)(2,1)S(1)}, u32[]{:S(2)}, u32[]{:S(2)}) collective-permute-start(bf16[512,128]{1,0:T(8,128)(2,1)S(1)} %get-tuple-element.19), channel_id=1, source_target_pairs={{0,8},{8,16},{16,24},{24,28},{28,20},{20,12},{12,4},{4,0},{1,9},{9... | collective-permute-start | bytes 393224 | tf_op jit(solution)/shard_map/ppermute | solution.py:215
  41.2 5.0 %collective-permute-start.34 = (bf16[512,128]{1,0:T(8,128)(2,1)S(1)}, bf16[512,128]{1,0:T(8,128)(2,1)S(1)}, u32[]{:S(2)}, u32[]{:S(2)}) collective-permute-start(bf16[512,128]{1,0:T(8,128)(2,1)S(1)} %get-tuple-element.18), channel_id=1, source_target_pairs={{8,0},{16,8},{24,16},{28,24},{20,28},{12,20},{4,12},{0,4},{9,1},{1... | collective-permute-start | bytes 393224 | tf_op jit(solution)/shard_map/ppermute | solution.py:215
  42.8 5.0 %collective-permute-start.4 = (bf16[512,128]{1,0:T(8,128)(2,1)S(1)}, bf16[512,128]{1,0:T(8,128)(2,1)S(1)}, u32[]{:S(2)}, u32[]{:S(2)}) collective-permute-start(bf16[512,128]{1,0:T(8,128)(2,1)S(1)} %get-tuple-element.17), channel_id=1, source_target_pairs={{0,8},{8,16},{16,24},{24,28},{28,20},{20,12},{12,4},{4,0},{1,9},{9... | collective-permute-start | bytes 393224 | tf_op jit(solution)/shard_map/ppermute | solution.py:215
  47.8 6.4 %collective-permute-start.15 = (bf16[512,128]{1,0:T(8,128)(2,1)S(1)}, bf16[512,128]{1,0:T(8,128)(2,1)S(1)}, u32[]{:S(2)}, u32[]{:S(2)}) collective-permute-start(bf16[512,128]{1,0:T(8,128)(2,1)S(1)} %get-tuple-element.16), channel_id=1, source_target_pairs={{8,0},{16,8},{24,16},{28,24},{20,28},{12,20},{4,12},{0,4},{9,1},{1... | collective-permute-start | bytes 393224 | tf_op jit(solution)/shard_map/ppermute | solution.py:215
  49.4 6.4 %collective-permute-start.25 = (bf16[512,128]{1,0:T(8,128)(2,1)S(1)}, bf16[512,128]{1,0:T(8,128)(2,1)S(1)}, u32[]{:S(2)}, u32[]{:S(2)}) collective-permute-start(bf16[512,128]{1,0:T(8,128)(2,1)S(1)} %get-tuple-element.15), channel_id=1, source_target_pairs={{0,8},{8,16},{16,24},{24,28},{28,20},{20,12},{12,4},{4,0},{1,9},{9... | collective-permute-start | bytes 393224 | tf_op jit(solution)/shard_map/ppermute | solution.py:215
  49.9 7.1 %collective-permute-start.35 = (bf16[512,128]{1,0:T(8,128)(2,1)S(1)}, bf16[512,128]{1,0:T(8,128)(2,1)S(1)}, u32[]{:S(2)}, u32[]{:S(2)}) collective-permute-start(bf16[512,128]{1,0:T(8,128)(2,1)S(1)} %get-tuple-element.14), channel_id=1, source_target_pairs={{8,0},{16,8},{24,16},{28,24},{20,28},{12,20},{4,12},{0,4},{9,1},{1... | collective-permute-start | bytes 393224 | tf_op jit(solution)/shard_map/ppermute | solution.py:215
  51.5 7.1 %collective-permute-start.5 = (bf16[512,128]{1,0:T(8,128)(2,1)S(1)}, bf16[512,128]{1,0:T(8,128)(2,1)S(1)}, u32[]{:S(2)}, u32[]{:S(2)}) collective-permute-start(bf16[512,128]{1,0:T(8,128)(2,1)S(1)} %get-tuple-element.13), channel_id=1, source_target_pairs={{0,8},{8,16},{16,24},{24,28},{28,20},{20,12},{12,4},{4,0},{1,9},{9... | collective-permute-start | bytes 393224 | tf_op jit(solution)/shard_map/ppermute | solution.py:215
  54.2 5.8 %collective-permute-start.16 = (bf16[512,128]{1,0:T(8,128)(2,1)S(1)}, bf16[512,128]{1,0:T(8,128)(2,1)S(1)}, u32[]{:S(2)}, u32[]{:S(2)}) collective-permute-start(bf16[512,128]{1,0:T(8,128)(2,1)S(1)} %collective-permute-done.15), channel_id=1, source_target_pairs={{8,0},{16,8},{24,16},{28,24},{20,28},{12,20},{4,12},{0,4},{9,1},{1... | collective-permute-start | bytes 393224 | tf_op jit(solution)/shard_map/ppermute | solution.py:215
  55.8 6.1 %collective-permute-start.26 = (bf16[512,128]{1,0:T(8,128)(2,1)S(1)}, bf16[512,128]{1,0:T(8,128)(2,1)S(1)}, u32[]{:S(2)}, u32[]{:S(2)}) collective-permute-start(bf16[512,128]{1,0:T(8,128)(2,1)S(1)} %collective-permute-done.25), channel_id=1, source_target_pairs={{0,8},{8,16},{16,24},{24,28},{28,20},{20,12},{12,4},{4,0},{1,9},{9... | collective-permute-start | bytes 393224 | tf_op jit(solution)/shard_map/ppermute | solution.py:215
  57.0 6.4 %collective-permute-start.36 = (bf16[512,128]{1,0:T(8,128)(2,1)S(1)}, bf16[512,128]{1,0:T(8,128)(2,1)S(1)}, u32[]{:S(2)}, u32[]{:S(2)}) collective-permute-start(bf16[512,128]{1,0:T(8,128)(2,1)S(1)} %collective-permute-done.35), channel_id=1, source_target_pairs={{8,0},{16,8},{24,16},{28,24},{20,28},{12,20},{4,12},{0,4},{9,1},{1... | collective-permute-start | bytes 393224 | tf_op jit(solution)/shard_map/ppermute | solution.py:215
  58.6 6.5 %collective-permute-start.6 = (bf16[512,128]{1,0:T(8,128)(2,1)S(1)}, bf16[512,128]{1,0:T(8,128)(2,1)S(1)}, u32[]{:S(2)}, u32[]{:S(2)}) collective-permute-start(bf16[512,128]{1,0:T(8,128)(2,1)S(1)} %collective-permute-done.5), channel_id=1, source_target_pairs={{0,8},{8,16},{16,24},{24,28},{28,20},{20,12},{12,4},{4,0},{1,9},{9... | collective-permute-start | bytes 393224 | tf_op jit(solution)/shard_map/ppermute | solution.py:215
  59.9 6.3 %collective-permute-start.17 = (bf16[512,128]{1,0:T(8,128)(2,1)S(1)}, bf16[512,128]{1,0:T(8,128)(2,1)S(1)}, u32[]{:S(2)}, u32[]{:S(2)}) collective-permute-start(bf16[512,128]{1,0:T(8,128)(2,1)S(1)} %collective-permute-done.16), channel_id=1, source_target_pairs={{8,0},{16,8},{24,16},{28,24},{20,28},{12,20},{4,12},{0,4},{9,1},{1... | collective-permute-start | bytes 393224 | tf_op jit(solution)/shard_map/ppermute | solution.py:215
  61.9 6.0 %collective-permute-start.27 = (bf16[512,128]{1,0:T(8,128)(2,1)S(1)}, bf16[512,128]{1,0:T(8,128)(2,1)S(1)}, u32[]{:S(2)}, u32[]{:S(2)}) collective-permute-start(bf16[512,128]{1,0:T(8,128)(2,1)S(1)} %collective-permute-done.26), channel_id=1, source_target_pairs={{0,8},{8,16},{16,24},{24,28},{28,20},{20,12},{12,4},{4,0},{1,9},{9... | collective-permute-start | bytes 393224 | tf_op jit(solution)/shard_map/ppermute | solution.py:215
  63.4 5.8 %collective-permute-start.37 = (bf16[512,128]{1,0:T(8,128)(2,1)S(1)}, bf16[512,128]{1,0:T(8,128)(2,1)S(1)}, u32[]{:S(2)}, u32[]{:S(2)}) collective-permute-start(bf16[512,128]{1,0:T(8,128)(2,1)S(1)} %collective-permute-done.36), channel_id=1, source_target_pairs={{8,0},{16,8},{24,16},{28,24},{20,28},{12,20},{4,12},{0,4},{9,1},{1... | collective-permute-start | bytes 393224 | tf_op jit(solution)/shard_map/ppermute | solution.py:215
  65.1 5.7 %collective-permute-start.7 = (bf16[512,128]{1,0:T(8,128)(2,1)S(1)}, bf16[512,128]{1,0:T(8,128)(2,1)S(1)}, u32[]{:S(2)}, u32[]{:S(2)}) collective-permute-start(bf16[512,128]{1,0:T(8,128)(2,1)S(1)} %collective-permute-done.6), channel_id=1, source_target_pairs={{0,8},{8,16},{16,24},{24,28},{28,20},{20,12},{12,4},{4,0},{1,9},{9... | collective-permute-start | bytes 393224 | tf_op jit(solution)/shard_map/ppermute | solution.py:215
  66.3 6.4 %collective-permute-start.18 = (bf16[512,128]{1,0:T(8,128)(2,1)S(1)}, bf16[512,128]{1,0:T(8,128)(2,1)S(1)}, u32[]{:S(2)}, u32[]{:S(2)}) collective-permute-start(bf16[512,128]{1,0:T(8,128)(2,1)S(1)} %collective-permute-done.17), channel_id=1, source_target_pairs={{8,0},{16,8},{24,16},{28,24},{20,28},{12,20},{4,12},{0,4},{9,1},{1... | collective-permute-start | bytes 393224 | tf_op jit(solution)/shard_map/ppermute | solution.py:215
  67.9 6.4 %collective-permute-start.28 = (bf16[512,128]{1,0:T(8,128)(2,1)S(1)}, bf16[512,128]{1,0:T(8,128)(2,1)S(1)}, u32[]{:S(2)}, u32[]{:S(2)}) collective-permute-start(bf16[512,128]{1,0:T(8,128)(2,1)S(1)} %collective-permute-done.27), channel_id=1, source_target_pairs={{0,8},{8,16},{16,24},{24,28},{28,20},{20,12},{12,4},{4,0},{1,9},{9... | collective-permute-start | bytes 393224 | tf_op jit(solution)/shard_map/ppermute | solution.py:215
  69.2 6.4 %collective-permute-start.38 = (bf16[512,128]{1,0:T(8,128)(2,1)S(1)}, bf16[512,128]{1,0:T(8,128)(2,1)S(1)}, u32[]{:S(2)}, u32[]{:S(2)}) collective-permute-start(bf16[512,128]{1,0:T(8,128)(2,1)S(1)} %collective-permute-done.37), channel_id=1, source_target_pairs={{8,0},{16,8},{24,16},{28,24},{20,28},{12,20},{4,12},{0,4},{9,1},{1... | collective-permute-start | bytes 393224 | tf_op jit(solution)/shard_map/ppermute | solution.py:215
  70.8 6.4 %collective-permute-start.8 = (bf16[512,128]{1,0:T(8,128)(2,1)S(1)}, bf16[512,128]{1,0:T(8,128)(2,1)S(1)}, u32[]{:S(2)}, u32[]{:S(2)}) collective-permute-start(bf16[512,128]{1,0:T(8,128)(2,1)S(1)} %collective-permute-done.7), channel_id=1, source_target_pairs={{0,8},{8,16},{16,24},{24,28},{28,20},{20,12},{12,4},{4,0},{1,9},{9... | collective-permute-start | bytes 393224 | tf_op jit(solution)/shard_map/ppermute | solution.py:215
  72.7 6.4 %collective-permute-start.19 = (bf16[512,128]{1,0:T(8,128)(2,1)S(1)}, bf16[512,128]{1,0:T(8,128)(2,1)S(1)}, u32[]{:S(2)}, u32[]{:S(2)}) collective-permute-start(bf16[512,128]{1,0:T(8,128)(2,1)S(1)} %collective-permute-done.18), channel_id=1, source_target_pairs={{8,0},{16,8},{24,16},{28,24},{20,28},{12,20},{4,12},{0,4},{9,1},{1... | collective-permute-start | bytes 393224 | tf_op jit(solution)/shard_map/ppermute | solution.py:215
  74.3 6.3 %collective-permute-start.29 = (bf16[512,128]{1,0:T(8,128)(2,1)S(1)}, bf16[512,128]{1,0:T(8,128)(2,1)S(1)}, u32[]{:S(2)}, u32[]{:S(2)}) collective-permute-start(bf16[512,128]{1,0:T(8,128)(2,1)S(1)} %collective-permute-done.28), channel_id=1, source_target_pairs={{0,8},{8,16},{16,24},{24,28},{28,20},{20,12},{12,4},{4,0},{1,9},{9... | collective-permute-start | bytes 393224 | tf_op jit(solution)/shard_map/ppermute | solution.py:215
  75.6 6.2 %collective-permute-start.39 = (bf16[512,128]{1,0:T(8,128)(2,1)S(1)}, bf16[512,128]{1,0:T(8,128)(2,1)S(1)}, u32[]{:S(2)}, u32[]{:S(2)}) collective-permute-start(bf16[512,128]{1,0:T(8,128)(2,1)S(1)} %collective-permute-done.38), channel_id=1, source_target_pairs={{8,0},{16,8},{24,16},{28,24},{20,28},{12,20},{4,12},{0,4},{9,1},{1... | collective-permute-start | bytes 393224 | tf_op jit(solution)/shard_map/ppermute | solution.py:215
  77.2 6.3 %collective-permute-start.9 = (bf16[512,128]{1,0:T(8,128)(2,1)S(1)}, bf16[512,128]{1,0:T(8,128)(2,1)S(1)}, u32[]{:S(2)}, u32[]{:S(2)}) collective-permute-start(bf16[512,128]{1,0:T(8,128)(2,1)S(1)} %collective-permute-done.8), channel_id=1, source_target_pairs={{0,8},{8,16},{16,24},{24,28},{28,20},{20,12},{12,4},{4,0},{1,9},{9... | collective-permute-start | bytes 393224 | tf_op jit(solution)/shard_map/ppermute | solution.py:215
  79.0 5.0 %collective-permute-start.20 = (bf16[512,128]{1,0:T(8,128)(2,1)S(1)}, bf16[512,128]{1,0:T(8,128)(2,1)S(1)}, u32[]{:S(2)}, u32[]{:S(2)}) collective-permute-start(bf16[512,128]{1,0:T(8,128)(2,1)S(1)} %collective-permute-done.19), channel_id=1, source_target_pairs={{8,0},{16,8},{24,16},{28,24},{20,28},{12,20},{4,12},{0,4},{9,1},{1... | collective-permute-start | bytes 393224 | tf_op jit(solution)/shard_map/ppermute | solution.py:215
  80.6 5.0 %collective-permute-start.30 = (bf16[512,128]{1,0:T(8,128)(2,1)S(1)}, bf16[512,128]{1,0:T(8,128)(2,1)S(1)}, u32[]{:S(2)}, u32[]{:S(2)}) collective-permute-start(bf16[512,128]{1,0:T(8,128)(2,1)S(1)} %collective-permute-done.29), channel_id=1, source_target_pairs={{0,8},{8,16},{16,24},{24,28},{28,20},{20,12},{12,4},{4,0},{1,9},{9... | collective-permute-start | bytes 393224 | tf_op jit(solution)/shard_map/ppermute | solution.py:215
  81.8 5.0 %collective-permute-start.40 = (bf16[512,128]{1,0:T(8,128)(2,1)S(1)}, bf16[512,128]{1,0:T(8,128)(2,1)S(1)}, u32[]{:S(2)}, u32[]{:S(2)}) collective-permute-start(bf16[512,128]{1,0:T(8,128)(2,1)S(1)} %collective-permute-done.39), channel_id=1, source_target_pairs={{8,0},{16,8},{24,16},{28,24},{20,28},{12,20},{4,12},{0,4},{9,1},{1... | collective-permute-start | bytes 393224 | tf_op jit(solution)/shard_map/ppermute | solution.py:215
  83.5 5.0 %collective-permute-start.10 = (bf16[512,128]{1,0:T(8,128)(2,1)S(1)}, bf16[512,128]{1,0:T(8,128)(2,1)S(1)}, u32[]{:S(2)}, u32[]{:S(2)}) collective-permute-start(bf16[512,128]{1,0:T(8,128)(2,1)S(1)} %collective-permute-done.9), channel_id=1, source_target_pairs={{0,8},{8,16},{16,24},{24,28},{28,20},{20,12},{12,4},{4,0},{1,9},{9... | collective-permute-start | bytes 393224 | tf_op jit(solution)/shard_map/ppermute | solution.py:215
  84.0 5.0 %collective-permute-start.21 = (bf16[512,128]{1,0:T(8,128)(2,1)S(1)}, bf16[512,128]{1,0:T(8,128)(2,1)S(1)}, u32[]{:S(2)}, u32[]{:S(2)}) collective-permute-start(bf16[512,128]{1,0:T(8,128)(2,1)S(1)} %collective-permute-done.20), channel_id=1, source_target_pairs={{8,0},{16,8},{24,16},{28,24},{20,28},{12,20},{4,12},{0,4},{9,1},{1... | collective-permute-start | bytes 393224 | tf_op jit(solution)/shard_map/ppermute | solution.py:215
  85.7 5.0 %collective-permute-start.31 = (bf16[512,128]{1,0:T(8,128)(2,1)S(1)}, bf16[512,128]{1,0:T(8,128)(2,1)S(1)}, u32[]{:S(2)}, u32[]{:S(2)}) collective-permute-start(bf16[512,128]{1,0:T(8,128)(2,1)S(1)} %collective-permute-done.30), channel_id=1, source_target_pairs={{0,8},{8,16},{16,24},{24,28},{28,20},{20,12},{12,4},{4,0},{1,9},{9... | collective-permute-start | bytes 393224 | tf_op jit(solution)/shard_map/ppermute | solution.py:215
  86.8 5.0 %collective-permute-start.41 = (bf16[512,128]{1,0:T(8,128)(2,1)S(1)}, bf16[512,128]{1,0:T(8,128)(2,1)S(1)}, u32[]{:S(2)}, u32[]{:S(2)}) collective-permute-start(bf16[512,128]{1,0:T(8,128)(2,1)S(1)} %collective-permute-done.40), channel_id=1, source_target_pairs={{8,0},{16,8},{24,16},{28,24},{20,28},{12,20},{4,12},{0,4},{9,1},{1... | collective-permute-start | bytes 393224 | tf_op jit(solution)/shard_map/ppermute | solution.py:215
  88.5 5.0 %collective-permute-start.11 = (bf16[512,128]{1,0:T(8,128)(2,1)S(1)}, bf16[512,128]{1,0:T(8,128)(2,1)S(1)}, u32[]{:S(2)}, u32[]{:S(2)}) collective-permute-start(bf16[512,128]{1,0:T(8,128)(2,1)S(1)} %collective-permute-done.10), channel_id=1, source_target_pairs={{0,8},{8,16},{16,24},{24,28},{28,20},{20,12},{12,4},{4,0},{1,9},{9... | collective-permute-start | bytes 393224 | tf_op jit(solution)/shard_map/ppermute | solution.py:215
  93.9 0.9 copy-start
  94.0 0.9 copy-start.1
  94.9 51.4 %copy-start.3 = (f32[6]{0:T(128)S(1)}, f32[6]{0:T(128)}, u32[]{:S(2)}) copy-start(f32[6]{0:T(128)} %param.15) | copy-start | bytes 76
  94.9 51.4 %copy-start.4 = (f32[2]{0:T(128)S(1)}, f32[2]{0:T(128)}, u32[]{:S(2)}) copy-start(f32[2]{0:T(128)} %param.14) | copy-start | bytes 28
  143.4 1.4 collective-permute-start.42
  144.8 5.4 %collective-permute-start.43 = (f32[24,1280]{1,0:T(8,128)S(1)}, f32[24,1280]{1,0:T(8,128)S(1)}, u32[]{:S(2)}, u32[]{:S(2)}) collective-permute-start(f32[24,1280]{1,0:T(8,128)S(1)} %add.228), channel_id=1, source_target_pairs={{0,2},{1,3},{2,0},{3,1},{4,6},{5,7},{6,4},{7,5},{8,10},{9,11},{10,... | collective-permute-start | bytes 368648 | tf_op jit(solution)/shard_map/ppermute | solution.py:284
